TPU v7x, 256 devices: a whole 4x4x8 slice. The times are simulated.
256 devices in a mesh: dp: 4 (over y_lo, core), ctx: 64 (over y_hi, x, z).
Axes of the slice: x: 4, y: 4 (y_hi: 2, y_lo: 2; y = y_hi * 2 + y_lo), z: 8, core: 2. Of those that a mesh axis runs over, the one named last changes fastest.
Arguments:
- query: bfloat16 [4, 16384, 4096], P('dp', 'ctx'), may hold values from -6 to 6
- key_proj: bfloat16 [4, 16384, 512], P('dp', 'ctx'), may hold values from -6 to 6
- value: bfloat16 [4, 16384, 512], P('dp', 'ctx'), may hold values from -6 to 6
- sinks: float32 [64], replicated, may hold values from 0 to 6
- doc_ids: int32 [4, 16384], P('dp'), may hold values from 0 to 63, never falling along the last dimension, each value on 1 to 512 neighbouring positions
- grad_out: bfloat16 [4, 16384, 4096], P('dp', 'ctx'), may hold values from -6 to 6
Outputs:
- attended: bfloat16 [4, 16384, 4096], P('dp', 'ctx')
- grad_query: bfloat16 [4, 16384, 4096], P('dp', 'ctx')
- grad_key: bfloat16 [4, 16384, 512], P('dp', 'ctx')
- grad_value: bfloat16 [4, 16384, 512], P('dp', 'ctx')
- grad_sinks: float32 [64], replicated
Inputs may be any that keep to these rules, and one draw needn't show every extreme that they name: `doc_ids`: each trace's documents are contiguous runs of tokens, numbered upward, each at most 512 tokens long, one exactly so.
All inputs are finite; a program needn't handle non-finite values.
Results may differ from a plain program's by a relative error of at most 0.012.
The roundings to bfloat16 on the way count: a program that leaves them out, or rounds other values in their place, can miss the bound.
Values may be sent and summed in bfloat16 or wider, within the bound.
No kernel may reach another device: no remote copies, remote signals or barrier semaphores. Data moves between devices by JAX's collectives and lax.ppermute only.
A program may use at most 128 MiB of HBM per device.

v0:
```python
import jax
import jax.numpy as jnp
from jax import lax
from jax.sharding import PartitionSpec as P

H = 64
KV = 8
HD = 64
SPAN = 2


score_scale = 0.125


def passed_along(block, axis, distance):
    devices = range(lax.axis_size(axis))
    route = [(i - distance, i) for i in devices if i - distance in devices]
    return lax.ppermute(block, axis, route)


def head_block(items, visible):
    q_head, k_head, v_head, g_head, sink_head = items
    scores = (
        jnp.einsum("gtd,ld->gtl", q_head, k_head, preferred_element_type=jnp.float32) * score_scale
    )
    scores = jnp.where(visible[None], scores, -jnp.inf)
    top = jnp.maximum(jnp.max(scores, axis=-1), sink_head[:, None])
    expo = jnp.exp(scores - top[..., None])
    sink_part = jnp.exp(sink_head[:, None] - top)
    denom = jnp.sum(expo, axis=-1) + sink_part
    probs = expo / denom[..., None]
    weights = probs.astype(jnp.bfloat16)
    attended = jnp.einsum(
        "gtl,ld->gtd", weights, v_head, preferred_element_type=jnp.float32
    ).astype(jnp.bfloat16)
    rowdot = jnp.sum(g_head.astype(jnp.float32) * attended.astype(jnp.float32), axis=-1)
    dprobs = jnp.einsum("gtd,ld->gtl", g_head, v_head, preferred_element_type=jnp.float32)
    score_grads = (probs * (dprobs - rowdot[..., None])).astype(jnp.bfloat16)
    grad_q = (
        jnp.einsum("gtl,ld->gtd", score_grads, k_head, preferred_element_type=jnp.float32)
        * score_scale
    ).astype(jnp.bfloat16)
    grad_k = (
        jnp.einsum("gtl,gtd->ld", score_grads, q_head, preferred_element_type=jnp.float32)
        * score_scale
    )
    grad_v = jnp.einsum("gtl,gtd->ld", weights, g_head, preferred_element_type=jnp.float32)
    sink_grad = -jnp.sum(sink_part / denom * rowdot, axis=-1)
    return (attended, grad_q, grad_k, grad_v, sink_grad)


def attend(queries, keys_win, values_win, grads, sinks, visible):
    rows = queries.shape[0]
    width = keys_win.shape[0]
    groups = H // KV
    q_heads = queries.reshape(rows, KV, groups, HD).transpose(1, 2, 0, 3)
    g_heads = grads.reshape(rows, KV, groups, HD).transpose(1, 2, 0, 3)
    k_heads = keys_win.reshape(width, KV, HD).transpose(1, 0, 2)
    v_heads = values_win.reshape(width, KV, HD).transpose(1, 0, 2)
    sink_heads = sinks.reshape(KV, groups)
    attended, grad_q, grad_k, grad_v, sink_grad = lax.map(
        lambda items: head_block(items, visible), (q_heads, k_heads, v_heads, g_heads, sink_heads)
    )
    attended = attended.transpose(2, 0, 1, 3).reshape(rows, H * HD)
    grad_q = grad_q.transpose(2, 0, 1, 3).reshape(rows, H * HD)
    grad_k = grad_k.transpose(1, 0, 2).reshape(width, KV * HD)
    grad_v = grad_v.transpose(1, 0, 2).reshape(width, KV * HD)
    return (attended, grad_q, grad_k, grad_v, sink_grad.reshape(H))


def on_device(query, key_proj, value, sinks, doc_ids, grad_out):
    queries = query[0]
    keys_own = key_proj[0]
    values_own = value[0]
    grads = grad_out[0]
    block_rows = queries.shape[0]
    width = (SPAN + 1) * block_rows
    front = SPAN * block_rows
    position = lax.axis_index("ctx")
    earlier = []
    for offset in range(1, SPAN + 1):
        earlier.append(passed_along((keys_own, values_own), "ctx", offset))
    keys_win = jnp.concatenate(
        [earlier[SPAN - 1 - index][0] for index in range(SPAN)] + [keys_own], axis=0
    )
    values_win = jnp.concatenate(
        [earlier[SPAN - 1 - index][1] for index in range(SPAN)] + [values_own], axis=0
    )
    seg_pad = jnp.concatenate([jnp.full((front,), -1, jnp.int32), doc_ids[0]], axis=0)
    start = position * block_rows
    q_seg = lax.dynamic_slice_in_dim(seg_pad, start + front, block_rows)
    k_seg = lax.dynamic_slice_in_dim(seg_pad, start, width)
    k_pos = start - front + jnp.arange(width, dtype=jnp.int32)
    q_pos = start + jnp.arange(block_rows, dtype=jnp.int32)
    visible = (
        (q_seg[:, None] == k_seg[None, :])
        & (k_pos[None, :] <= q_pos[:, None])
        & (k_pos[None, :] >= 0)
    )
    attended, grad_q, grad_k, grad_v, sink_grad = attend(
        queries, keys_win, values_win, grads, sinks, visible
    )
    total_k = grad_k[front:]
    total_v = grad_v[front:]
    for offset in range(1, SPAN + 1):
        lower = (SPAN - offset) * block_rows
        got_k, got_v = (
            passed_along(
                grad_k[lower : lower + block_rows].astype(jnp.bfloat16), "ctx", -offset
            ).astype(jnp.float32),
            passed_along(
                grad_v[lower : lower + block_rows].astype(jnp.bfloat16), "ctx", -offset
            ).astype(jnp.float32),
        )
        total_k = total_k + got_k
        total_v = total_v + got_v
    sink_total = lax.psum(sink_grad, ("dp", "ctx"))
    return (
        attended[None],
        grad_q[None],
        total_k.astype(jnp.bfloat16)[None],
        total_v.astype(jnp.bfloat16)[None],
        sink_total,
    )


def solution(mesh):
    in_specs = (
        P("dp", "ctx", None),
        P("dp", "ctx", None),
        P("dp", "ctx", None),
        P(),
        P("dp", None),
        P("dp", "ctx", None),
    )
    out_specs = (
        P("dp", "ctx", None),
        P("dp", "ctx", None),
        P("dp", "ctx", None),
        P("dp", "ctx", None),
        P(),
    )
    return jax.shard_map(
        on_device, mesh=mesh, in_specs=in_specs, out_specs=out_specs, check_vma=False
    )
```

profile of v0, /device:TPU:1, one launch (start us, length us, event | category | flops | bytes accessed | tf_op | source)
XLA Modules:
  0.0 325.8 jit_solution(18019898556537907129)
XLA Ops:
  0.6 6.5 %collective-permute-start = (bf16[256,512]{1,0:T(8,128)(2,1)}, bf16[256,512]{1,0:T(8,128)(2,1)}, u32[]{:S(2)}, u32[]{:S(2)}) collective-permute-start(bf16[256,512]{1,0:T(8,128)(2,1)} %bitcast.157), channel_id=1, source_target_pairs={{0,2},{1,3},{2,4},{3,5},{4,6},{5,7},{6,8},{7,9},{8,10},{9,11},{10,... | collective-permute-start | bytes 786440 | tf_op jit(solution)/shard_map/ppermute | solution.py:18
  7.1 3.5 %collective-permute-start.1 = (bf16[256,512]{1,0:T(8,128)(2,1)}, bf16[256,512]{1,0:T(8,128)(2,1)S(1)}, u32[]{:S(2)}, u32[]{:S(2)}) collective-permute-start(bf16[256,512]{1,0:T(8,128)(2,1)} %bitcast.158), channel_id=1, source_target_pairs={{0,1},{1,2},{2,3},{3,4},{4,5},{5,6},{6,7},{7,8},{8,9},{9,10},{10,1... | collective-permute-start | bytes 786440 | tf_op jit(solution)/shard_map/ppermute | solution.py:18
  10.7 4.5 %collective-permute-start.2 = (bf16[256,512]{1,0:T(8,128)(2,1)}, bf16[256,512]{1,0:T(8,128)(2,1)S(1)}, u32[]{:S(2)}, u32[]{:S(2)}) collective-permute-start(bf16[256,512]{1,0:T(8,128)(2,1)} %bitcast.159), channel_id=1, source_target_pairs={{0,2},{1,3},{2,4},{3,5},{4,6},{5,7},{6,8},{7,9},{8,10},{9,11},{10,... | collective-permute-start | bytes 786440 | tf_op jit(solution)/shard_map/ppermute | solution.py:18
  15.2 2.7 collective-permute-start.3
  20.1 3.3 %copy.27 = bf16[1,256,4096]{1,2,0:T(8,128)(2,1)S(1)} copy(bf16[1,256,4096]{2,1,0:T(8,128)(2,1)} %param.8) | data formatting | bytes 4194304 | tf_op args[0]
  23.4 4.1 %copy.34 = bf16[1,256,4096]{1,2,0:T(8,128)(2,1)} copy(bf16[1,256,4096]{2,1,0:T(8,128)(2,1)} %param.13) | data formatting | bytes 4194304 | tf_op args[5]
  27.7 1.8 copy.28
  31.3 8.5 %collective-permute-done.3 = bf16[256,512]{1,0:T(8,128)(2,1)S(1)} collective-permute-done((bf16[256,512]{1,0:T(8,128)(2,1)}, bf16[256,512]{1,0:T(8,128)(2,1)S(1)}, u32[]{:S(2)}, u32[]{:S(2)}) %collective-permute-start.3) | collective-permute-done | bytes 262176 | tf_op jit(solution)/shard_map/ppermute | solution.py:18
  40.7 2.2 maximum_bitcast_fusion
  42.9 171.0 %while.19 = (s32[]{:T(128)}, bf16[8,8,256,64]{2,3,1,0:T(8,128)(2,1)}, bf16[8,8,256,64]{2,3,1,0:T(8,128)(2,1)}, f32[8,768,64]{1,2,0:T(8,128)}, f32[8,768,64]{1,2,...) while((s32[]{:T(128)}, ...), condition=%wide.region_5.6_spmd.clone, body=%wide.region_0.5_spmd.clone.sunk | while | flops 1247475712 | bytes 106208632 | solution.py:61
  44.5 1.6 fusion.84
  47.0 3.7 %bitcast_dynamic-update-slice_fusion.2 = (bf16[8,8,256,64]{2,3,1,0:T(8,128)(2,1)}, bf16[8,256,64]{1,2,0:T(8,128)(2,1)S(1)}) fusion(bf16[8,8,256,64]{2,3,1,0:T(8,128)(2,1)} %get-tuple-element.290, s32[]{:T(128)} %get-tuple-element.289, bf16[8,768,64]{1,2,0:T(8,128)(2,1)} %get-tuple-element.316, f32[8,256]{1,0:T(8,128)S(1)} %fusion.85, ...), kind=kOutput, calls=%fused_computation.26.clone.1 | convolution fusion | flops 209321984 | bytes 7128064 | tf_op jit(solution)/shard_map/while/body/eval_jaxpr/gtl,ld->gtd/dot_general | solution.py:33
  52.2 5.5 %fusion.88 = f32[8,768,64]{1,2,0:T(8,128)} fusion(f32[8,768,64]{1,2,0:T(8,128)} %get-tuple-element.293, s32[]{:T(128)} %get-tuple-element.289, bf16[8,8,256,64]{2,3,1,0:T(8,128)(2,1)} %get-tuple-element.317, f32[8,256,768]{2,1,0:T(8,128)} %copy-done, f32[8,256]{1,0:T(8,128)S(1)} %fusion.85, f32[8,256]{1,0:T(8,128)S(1)} %broadcast_maximum_fusion.2, ...), kind=kOutput, calls=%fused_computation.17.clone.1 | convolution fusion | flops 209190912 | bytes 6964224 | tf_op jit(solution)/shard_map/while/body/eval_jaxpr/gtl,gtd->ld/dot_general | solution.py:47
  57.7 3.4 %multiply_convert_fusion.2 = bf16[8,256,768]{2,1,0:T(8,128)(2,1)S(1)} fusion(f32[8,256]{1,0:T(8,128)S(1)} %multiply_reduce_fusion.4, bf16[8,8,256,64]{2,3,1,0:T(8,128)(2,1)} %get-tuple-element.317, s32[]{:T(128)} %get-tuple-element.289, bf16[8,768,64]{1,2,0:T(8,128)(2,1)} %get-tuple-element.316, f32[8,256]{1,0:T(8,128)S(1)} %fusion.85, ...), kind=kOutput, calls=%fused_computation.1.clone.1 | convolution fusion | flops 212336640 | bytes 10019840 | tf_op jit(solution)/shard_map/while/body/eval_jaxpr/gtd,ld->gtl/dot_general | solution.py:37
  61.1 1.8 fusion.86
  65.9 1.6 fusion.84
  68.4 3.7 %bitcast_dynamic-update-slice_fusion.2 = (bf16[8,8,256,64]{2,3,1,0:T(8,128)(2,1)}, bf16[8,256,64]{1,2,0:T(8,128)(2,1)S(1)}) fusion(bf16[8,8,256,64]{2,3,1,0:T(8,128)(2,1)} %get-tuple-element.290, s32[]{:T(128)} %get-tuple-element.289, bf16[8,768,64]{1,2,0:T(8,128)(2,1)} %get-tuple-element.316, f32[8,256]{1,0:T(8,128)S(1)} %fusion.85, ...), kind=kOutput, calls=%fused_computation.26.clone.1 | convolution fusion | flops 209321984 | bytes 7128064 | tf_op jit(solution)/shard_map/while/body/eval_jaxpr/gtl,ld->gtd/dot_general | solution.py:33
  73.6 5.5 %fusion.88 = f32[8,768,64]{1,2,0:T(8,128)} fusion(f32[8,768,64]{1,2,0:T(8,128)} %get-tuple-element.293, s32[]{:T(128)} %get-tuple-element.289, bf16[8,8,256,64]{2,3,1,0:T(8,128)(2,1)} %get-tuple-element.317, f32[8,256,768]{2,1,0:T(8,128)} %copy-done, f32[8,256]{1,0:T(8,128)S(1)} %fusion.85, f32[8,256]{1,0:T(8,128)S(1)} %broadcast_maximum_fusion.2, ...), kind=kOutput, calls=%fused_computation.17.clone.1 | convolution fusion | flops 209190912 | bytes 6964224 | tf_op jit(solution)/shard_map/while/body/eval_jaxpr/gtl,gtd->ld/dot_general | solution.py:47
  79.1 3.4 %multiply_convert_fusion.2 = bf16[8,256,768]{2,1,0:T(8,128)(2,1)S(1)} fusion(f32[8,256]{1,0:T(8,128)S(1)} %multiply_reduce_fusion.4, bf16[8,8,256,64]{2,3,1,0:T(8,128)(2,1)} %get-tuple-element.317, s32[]{:T(128)} %get-tuple-element.289, bf16[8,768,64]{1,2,0:T(8,128)(2,1)} %get-tuple-element.316, f32[8,256]{1,0:T(8,128)S(1)} %fusion.85, ...), kind=kOutput, calls=%fused_computation.1.clone.1 | convolution fusion | flops 212336640 | bytes 10019840 | tf_op jit(solution)/shard_map/while/body/eval_jaxpr/gtd,ld->gtl/dot_general | solution.py:37
  82.5 1.8 fusion.86
  89.8 3.7 %bitcast_dynamic-update-slice_fusion.2 = (bf16[8,8,256,64]{2,3,1,0:T(8,128)(2,1)}, bf16[8,256,64]{1,2,0:T(8,128)(2,1)S(1)}) fusion(bf16[8,8,256,64]{2,3,1,0:T(8,128)(2,1)} %get-tuple-element.290, s32[]{:T(128)} %get-tuple-element.289, bf16[8,768,64]{1,2,0:T(8,128)(2,1)} %get-tuple-element.316, f32[8,256]{1,0:T(8,128)S(1)} %fusion.85, ...), kind=kOutput, calls=%fused_computation.26.clone.1 | convolution fusion | flops 209321984 | bytes 7128064 | tf_op jit(solution)/shard_map/while/body/eval_jaxpr/gtl,ld->gtd/dot_general | solution.py:33
  95.0 5.5 %fusion.88 = f32[8,768,64]{1,2,0:T(8,128)} fusion(f32[8,768,64]{1,2,0:T(8,128)} %get-tuple-element.293, s32[]{:T(128)} %get-tuple-element.289, bf16[8,8,256,64]{2,3,1,0:T(8,128)(2,1)} %get-tuple-element.317, f32[8,256,768]{2,1,0:T(8,128)} %copy-done, f32[8,256]{1,0:T(8,128)S(1)} %fusion.85, f32[8,256]{1,0:T(8,128)S(1)} %broadcast_maximum_fusion.2, ...), kind=kOutput, calls=%fused_computation.17.clone.1 | convolution fusion | flops 209190912 | bytes 6964224 | tf_op jit(solution)/shard_map/while/body/eval_jaxpr/gtl,gtd->ld/dot_general | solution.py:47
  100.4 3.4 %multiply_convert_fusion.2 = bf16[8,256,768]{2,1,0:T(8,128)(2,1)S(1)} fusion(f32[8,256]{1,0:T(8,128)S(1)} %multiply_reduce_fusion.4, bf16[8,8,256,64]{2,3,1,0:T(8,128)(2,1)} %get-tuple-element.317, s32[]{:T(128)} %get-tuple-element.289, bf16[8,768,64]{1,2,0:T(8,128)(2,1)} %get-tuple-element.316, f32[8,256]{1,0:T(8,128)S(1)} %fusion.85, ...), kind=kOutput, calls=%fused_computation.1.clone.1 | convolution fusion | flops 212336640 | bytes 10019840 | tf_op jit(solution)/shard_map/while/body/eval_jaxpr/gtd,ld->gtl/dot_general | solution.py:37
  103.9 1.8 fusion.86
  111.2 3.7 %bitcast_dynamic-update-slice_fusion.2 = (bf16[8,8,256,64]{2,3,1,0:T(8,128)(2,1)}, bf16[8,256,64]{1,2,0:T(8,128)(2,1)S(1)}) fusion(bf16[8,8,256,64]{2,3,1,0:T(8,128)(2,1)} %get-tuple-element.290, s32[]{:T(128)} %get-tuple-element.289, bf16[8,768,64]{1,2,0:T(8,128)(2,1)} %get-tuple-element.316, f32[8,256]{1,0:T(8,128)S(1)} %fusion.85, ...), kind=kOutput, calls=%fused_computation.26.clone.1 | convolution fusion | flops 209321984 | bytes 7128064 | tf_op jit(solution)/shard_map/while/body/eval_jaxpr/gtl,ld->gtd/dot_general | solution.py:33
  116.3 5.5 %fusion.88 = f32[8,768,64]{1,2,0:T(8,128)} fusion(f32[8,768,64]{1,2,0:T(8,128)} %get-tuple-element.293, s32[]{:T(128)} %get-tuple-element.289, bf16[8,8,256,64]{2,3,1,0:T(8,128)(2,1)} %get-tuple-element.317, f32[8,256,768]{2,1,0:T(8,128)} %copy-done, f32[8,256]{1,0:T(8,128)S(1)} %fusion.85, f32[8,256]{1,0:T(8,128)S(1)} %broadcast_maximum_fusion.2, ...), kind=kOutput, calls=%fused_computation.17.clone.1 | convolution fusion | flops 209190912 | bytes 6964224 | tf_op jit(solution)/shard_map/while/body/eval_jaxpr/gtl,gtd->ld/dot_general | solution.py:47
  121.8 3.4 %multiply_convert_fusion.2 = bf16[8,256,768]{2,1,0:T(8,128)(2,1)S(1)} fusion(f32[8,256]{1,0:T(8,128)S(1)} %multiply_reduce_fusion.4, bf16[8,8,256,64]{2,3,1,0:T(8,128)(2,1)} %get-tuple-element.317, s32[]{:T(128)} %get-tuple-element.289, bf16[8,768,64]{1,2,0:T(8,128)(2,1)} %get-tuple-element.316, f32[8,256]{1,0:T(8,128)S(1)} %fusion.85, ...), kind=kOutput, calls=%fused_computation.1.clone.1 | convolution fusion | flops 212336640 | bytes 10019840 | tf_op jit(solution)/shard_map/while/body/eval_jaxpr/gtd,ld->gtl/dot_general | solution.py:37
  125.3 1.8 fusion.86
  132.5 3.7 %bitcast_dynamic-update-slice_fusion.2 = (bf16[8,8,256,64]{2,3,1,0:T(8,128)(2,1)}, bf16[8,256,64]{1,2,0:T(8,128)(2,1)S(1)}) fusion(bf16[8,8,256,64]{2,3,1,0:T(8,128)(2,1)} %get-tuple-element.290, s32[]{:T(128)} %get-tuple-element.289, bf16[8,768,64]{1,2,0:T(8,128)(2,1)} %get-tuple-element.316, f32[8,256]{1,0:T(8,128)S(1)} %fusion.85, ...), kind=kOutput, calls=%fused_computation.26.clone.1 | convolution fusion | flops 209321984 | bytes 7128064 | tf_op jit(solution)/shard_map/while/body/eval_jaxpr/gtl,ld->gtd/dot_general | solution.py:33
  137.7 5.5 %fusion.88 = f32[8,768,64]{1,2,0:T(8,128)} fusion(f32[8,768,64]{1,2,0:T(8,128)} %get-tuple-element.293, s32[]{:T(128)} %get-tuple-element.289, bf16[8,8,256,64]{2,3,1,0:T(8,128)(2,1)} %get-tuple-element.317, f32[8,256,768]{2,1,0:T(8,128)} %copy-done, f32[8,256]{1,0:T(8,128)S(1)} %fusion.85, f32[8,256]{1,0:T(8,128)S(1)} %broadcast_maximum_fusion.2, ...), kind=kOutput, calls=%fused_computation.17.clone.1 | convolution fusion | flops 209190912 | bytes 6964224 | tf_op jit(solution)/shard_map/while/body/eval_jaxpr/gtl,gtd->ld/dot_general | solution.py:47
  143.2 3.4 %multiply_convert_fusion.2 = bf16[8,256,768]{2,1,0:T(8,128)(2,1)S(1)} fusion(f32[8,256]{1,0:T(8,128)S(1)} %multiply_reduce_fusion.4, bf16[8,8,256,64]{2,3,1,0:T(8,128)(2,1)} %get-tuple-element.317, s32[]{:T(128)} %get-tuple-element.289, bf16[8,768,64]{1,2,0:T(8,128)(2,1)} %get-tuple-element.316, f32[8,256]{1,0:T(8,128)S(1)} %fusion.85, ...), kind=kOutput, calls=%fused_computation.1.clone.1 | convolution fusion | flops 212336640 | bytes 10019840 | tf_op jit(solution)/shard_map/while/body/eval_jaxpr/gtd,ld->gtl/dot_general | solution.py:37
  146.6 1.8 fusion.86
  153.9 3.7 %bitcast_dynamic-update-slice_fusion.2 = (bf16[8,8,256,64]{2,3,1,0:T(8,128)(2,1)}, bf16[8,256,64]{1,2,0:T(8,128)(2,1)S(1)}) fusion(bf16[8,8,256,64]{2,3,1,0:T(8,128)(2,1)} %get-tuple-element.290, s32[]{:T(128)} %get-tuple-element.289, bf16[8,768,64]{1,2,0:T(8,128)(2,1)} %get-tuple-element.316, f32[8,256]{1,0:T(8,128)S(1)} %fusion.85, ...), kind=kOutput, calls=%fused_computation.26.clone.1 | convolution fusion | flops 209321984 | bytes 7128064 | tf_op jit(solution)/shard_map/while/body/eval_jaxpr/gtl,ld->gtd/dot_general | solution.py:33
  159.1 5.5 %fusion.88 = f32[8,768,64]{1,2,0:T(8,128)} fusion(f32[8,768,64]{1,2,0:T(8,128)} %get-tuple-element.293, s32[]{:T(128)} %get-tuple-element.289, bf16[8,8,256,64]{2,3,1,0:T(8,128)(2,1)} %get-tuple-element.317, f32[8,256,768]{2,1,0:T(8,128)} %copy-done, f32[8,256]{1,0:T(8,128)S(1)} %fusion.85, f32[8,256]{1,0:T(8,128)S(1)} %broadcast_maximum_fusion.2, ...), kind=kOutput, calls=%fused_computation.17.clone.1 | convolution fusion | flops 209190912 | bytes 6964224 | tf_op jit(solution)/shard_map/while/body/eval_jaxpr/gtl,gtd->ld/dot_general | solution.py:47
  164.6 3.4 %multiply_convert_fusion.2 = bf16[8,256,768]{2,1,0:T(8,128)(2,1)S(1)} fusion(f32[8,256]{1,0:T(8,128)S(1)} %multiply_reduce_fusion.4, bf16[8,8,256,64]{2,3,1,0:T(8,128)(2,1)} %get-tuple-element.317, s32[]{:T(128)} %get-tuple-element.289, bf16[8,768,64]{1,2,0:T(8,128)(2,1)} %get-tuple-element.316, f32[8,256]{1,0:T(8,128)S(1)} %fusion.85, ...), kind=kOutput, calls=%fused_computation.1.clone.1 | convolution fusion | flops 212336640 | bytes 10019840 | tf_op jit(solution)/shard_map/while/body/eval_jaxpr/gtd,ld->gtl/dot_general | solution.py:37
  168.0 1.8 fusion.86
  175.3 3.7 %bitcast_dynamic-update-slice_fusion.2 = (bf16[8,8,256,64]{2,3,1,0:T(8,128)(2,1)}, bf16[8,256,64]{1,2,0:T(8,128)(2,1)S(1)}) fusion(bf16[8,8,256,64]{2,3,1,0:T(8,128)(2,1)} %get-tuple-element.290, s32[]{:T(128)} %get-tuple-element.289, bf16[8,768,64]{1,2,0:T(8,128)(2,1)} %get-tuple-element.316, f32[8,256]{1,0:T(8,128)S(1)} %fusion.85, ...), kind=kOutput, calls=%fused_computation.26.clone.1 | convolution fusion | flops 209321984 | bytes 7128064 | tf_op jit(solution)/shard_map/while/body/eval_jaxpr/gtl,ld->gtd/dot_general | solution.py:33
  180.4 5.5 %fusion.88 = f32[8,768,64]{1,2,0:T(8,128)} fusion(f32[8,768,64]{1,2,0:T(8,128)} %get-tuple-element.293, s32[]{:T(128)} %get-tuple-element.289, bf16[8,8,256,64]{2,3,1,0:T(8,128)(2,1)} %get-tuple-element.317, f32[8,256,768]{2,1,0:T(8,128)} %copy-done, f32[8,256]{1,0:T(8,128)S(1)} %fusion.85, f32[8,256]{1,0:T(8,128)S(1)} %broadcast_maximum_fusion.2, ...), kind=kOutput, calls=%fused_computation.17.clone.1 | convolution fusion | flops 209190912 | bytes 6964224 | tf_op jit(solution)/shard_map/while/body/eval_jaxpr/gtl,gtd->ld/dot_general | solution.py:47
  186.0 3.4 %multiply_convert_fusion.2 = bf16[8,256,768]{2,1,0:T(8,128)(2,1)S(1)} fusion(f32[8,256]{1,0:T(8,128)S(1)} %multiply_reduce_fusion.4, bf16[8,8,256,64]{2,3,1,0:T(8,128)(2,1)} %get-tuple-element.317, s32[]{:T(128)} %get-tuple-element.289, bf16[8,768,64]{1,2,0:T(8,128)(2,1)} %get-tuple-element.316, f32[8,256]{1,0:T(8,128)S(1)} %fusion.85, ...), kind=kOutput, calls=%fused_computation.1.clone.1 | convolution fusion | flops 212336640 | bytes 10019840 | tf_op jit(solution)/shard_map/while/body/eval_jaxpr/gtd,ld->gtl/dot_general | solution.py:37
  189.4 1.8 fusion.86
  196.7 3.7 %bitcast_dynamic-update-slice_fusion.2 = (bf16[8,8,256,64]{2,3,1,0:T(8,128)(2,1)}, bf16[8,256,64]{1,2,0:T(8,128)(2,1)S(1)}) fusion(bf16[8,8,256,64]{2,3,1,0:T(8,128)(2,1)} %get-tuple-element.290, s32[]{:T(128)} %get-tuple-element.289, bf16[8,768,64]{1,2,0:T(8,128)(2,1)} %get-tuple-element.316, f32[8,256]{1,0:T(8,128)S(1)} %fusion.85, ...), kind=kOutput, calls=%fused_computation.26.clone.1 | convolution fusion | flops 209321984 | bytes 7128064 | tf_op jit(solution)/shard_map/while/body/eval_jaxpr/gtl,ld->gtd/dot_general | solution.py:33
  201.8 5.5 %fusion.88 = f32[8,768,64]{1,2,0:T(8,128)} fusion(f32[8,768,64]{1,2,0:T(8,128)} %get-tuple-element.293, s32[]{:T(128)} %get-tuple-element.289, bf16[8,8,256,64]{2,3,1,0:T(8,128)(2,1)} %get-tuple-element.317, f32[8,256,768]{2,1,0:T(8,128)} %copy-done, f32[8,256]{1,0:T(8,128)S(1)} %fusion.85, f32[8,256]{1,0:T(8,128)S(1)} %broadcast_maximum_fusion.2, ...), kind=kOutput, calls=%fused_computation.17.clone.1 | convolution fusion | flops 209190912 | bytes 6964224 | tf_op jit(solution)/shard_map/while/body/eval_jaxpr/gtl,gtd->ld/dot_general | solution.py:47
  207.3 3.4 %multiply_convert_fusion.2 = bf16[8,256,768]{2,1,0:T(8,128)(2,1)S(1)} fusion(f32[8,256]{1,0:T(8,128)S(1)} %multiply_reduce_fusion.4, bf16[8,8,256,64]{2,3,1,0:T(8,128)(2,1)} %get-tuple-element.317, s32[]{:T(128)} %get-tuple-element.289, bf16[8,768,64]{1,2,0:T(8,128)(2,1)} %get-tuple-element.316, f32[8,256]{1,0:T(8,128)S(1)} %fusion.85, ...), kind=kOutput, calls=%fused_computation.1.clone.1 | convolution fusion | flops 212336640 | bytes 10019840 | tf_op jit(solution)/shard_map/while/body/eval_jaxpr/gtd,ld->gtl/dot_general | solution.py:37
  210.8 1.8 fusion.86
  213.9 1.6 bitcast_convert_fusion
  223.7 2.9 copy.35
  226.5 4.1 %copy.36 = bf16[1,256,4096]{2,1,0:T(8,128)(2,1)} copy(bf16[1,256,4096]{1,2,0:T(8,128)(2,1)} %bitcast.148) | data formatting | bytes 4194304
  230.7 91.2 %psum.7 = f32[64]{0:T(128)} all-reduce(f32[64]{0:T(128)S(1)} %reshape.126), channel_id=1, replica_groups=mesh['dp'=4,'ctx'=64] {'dp','ctx'}, use_global_device_ids=true, to_apply=%region_6.7 | all-reduce | flops 64 | bytes 512 | tf_op jit(solution)/shard_map/psum | solution.py:117
  (217 shorter events, 69.2 us)
Async XLA Ops:
  0.6 27.1 %collective-permute-start = (bf16[256,512]{1,0:T(8,128)(2,1)}, bf16[256,512]{1,0:T(8,128)(2,1)}, u32[]{:S(2)}, u32[]{:S(2)}) collective-permute-start(bf16[256,512]{1,0:T(8,128)(2,1)} %bitcast.157), channel_id=1, source_target_pairs={{0,2},{1,3},{2,4},{3,5},{4,6},{5,7},{6,8},{7,9},{8,10},{9,11},{10,... | collective-permute-start | bytes 786440 | tf_op jit(solution)/shard_map/ppermute | solution.py:18
  7.1 22.4 %collective-permute-start.1 = (bf16[256,512]{1,0:T(8,128)(2,1)}, bf16[256,512]{1,0:T(8,128)(2,1)S(1)}, u32[]{:S(2)}, u32[]{:S(2)}) collective-permute-start(bf16[256,512]{1,0:T(8,128)(2,1)} %bitcast.158), channel_id=1, source_target_pairs={{0,1},{1,2},{2,3},{3,4},{4,5},{5,6},{6,7},{7,8},{8,9},{9,10},{10,1... | collective-permute-start | bytes 786440 | tf_op jit(solution)/shard_map/ppermute | solution.py:18
  10.7 19.7 %collective-permute-start.2 = (bf16[256,512]{1,0:T(8,128)(2,1)}, bf16[256,512]{1,0:T(8,128)(2,1)S(1)}, u32[]{:S(2)}, u32[]{:S(2)}) collective-permute-start(bf16[256,512]{1,0:T(8,128)(2,1)} %bitcast.159), channel_id=1, source_target_pairs={{0,2},{1,3},{2,4},{3,5},{4,6},{5,7},{6,8},{7,9},{8,10},{9,11},{10,... | collective-permute-start | bytes 786440 | tf_op jit(solution)/shard_map/ppermute | solution.py:18
  15.2 24.6 %collective-permute-start.3 = (bf16[256,512]{1,0:T(8,128)(2,1)}, bf16[256,512]{1,0:T(8,128)(2,1)S(1)}, u32[]{:S(2)}, u32[]{:S(2)}) collective-permute-start(bf16[256,512]{1,0:T(8,128)(2,1)} %bitcast.160), channel_id=1, source_target_pairs={{0,1},{1,2},{2,3},{3,4},{4,5},{5,6},{6,7},{7,8},{8,9},{9,10},{10,1... | collective-permute-start | bytes 786440 | tf_op jit(solution)/shard_map/ppermute | solution.py:18
  20.1 7.4 %copy-start.6 = (f32[64]{0:T(128)S(1)}, f32[64]{0:T(128)}, u32[]{:S(2)}) copy-start(f32[64]{0:T(128)} %param.11) | copy-start | bytes 772
  23.4 4.2 %copy-start.5 = (s32[1,16384]{1,0:T(1,128)S(1)}, s32[1,16384]{1,0:T(1,128)}, u32[]{:S(2)}) copy-start(s32[1,16384]{1,0:T(1,128)} %param.12) | copy-start | bytes 196612
  44.4 2.7 copy-start
  50.8 6.9 %slice-start = ((s8[6291456]{0:T(1024)(128)(4,1)}), s8[2097152]{0:T(1024)(128)(4,1)S(1)}, s32[]{:S(2)}) async-start(s8[6291456]{0:T(1024)(128)(4,1)} %bitcast.141), calls=%async_computation | async-start | bytes 4194304 | tf_op jit(solution)/shard_map/while
  52.2 5.5 %slice-start.1 = ((s8[6291456]{0:T(1024)(128)(4,1)}), s8[4194304]{0:T(1024)(128)(4,1)S(1)}, s32[]{:S(2)}) async-start(s8[6291456]{0:T(1024)(128)(4,1)} %bitcast.141), calls=%async_computation.1 | async-start | bytes 8388608 | tf_op jit(solution)/shard_map/while
  61.1 1.8 copy-start.2
  64.3 1.5 copy-start.1
  65.8 2.7 copy-start
  72.2 6.9 %slice-start = ((s8[6291456]{0:T(1024)(128)(4,1)}), s8[2097152]{0:T(1024)(128)(4,1)S(1)}, s32[]{:S(2)}) async-start(s8[6291456]{0:T(1024)(128)(4,1)} %bitcast.141), calls=%async_computation | async-start | bytes 4194304 | tf_op jit(solution)/shard_map/while
  73.6 5.5 %slice-start.1 = ((s8[6291456]{0:T(1024)(128)(4,1)}), s8[4194304]{0:T(1024)(128)(4,1)S(1)}, s32[]{:S(2)}) async-start(s8[6291456]{0:T(1024)(128)(4,1)} %bitcast.141), calls=%async_computation.1 | async-start | bytes 8388608 | tf_op jit(solution)/shard_map/while
  82.5 1.8 copy-start.2
  87.1 2.7 copy-start
  93.5 6.9 %slice-start = ((s8[6291456]{0:T(1024)(128)(4,1)}), s8[2097152]{0:T(1024)(128)(4,1)S(1)}, s32[]{:S(2)}) async-start(s8[6291456]{0:T(1024)(128)(4,1)} %bitcast.141), calls=%async_computation | async-start | bytes 4194304 | tf_op jit(solution)/shard_map/while
  94.9 5.5 %slice-start.1 = ((s8[6291456]{0:T(1024)(128)(4,1)}), s8[4194304]{0:T(1024)(128)(4,1)S(1)}, s32[]{:S(2)}) async-start(s8[6291456]{0:T(1024)(128)(4,1)} %bitcast.141), calls=%async_computation.1 | async-start | bytes 8388608 | tf_op jit(solution)/shard_map/while
  103.9 1.8 copy-start.2
  107.0 1.5 copy-start.1
  108.5 2.7 copy-start
  114.9 6.9 %slice-start = ((s8[6291456]{0:T(1024)(128)(4,1)}), s8[2097152]{0:T(1024)(128)(4,1)S(1)}, s32[]{:S(2)}) async-start(s8[6291456]{0:T(1024)(128)(4,1)} %bitcast.141), calls=%async_computation | async-start | bytes 4194304 | tf_op jit(solution)/shard_map/while
  116.3 5.5 %slice-start.1 = ((s8[6291456]{0:T(1024)(128)(4,1)}), s8[4194304]{0:T(1024)(128)(4,1)S(1)}, s32[]{:S(2)}) async-start(s8[6291456]{0:T(1024)(128)(4,1)} %bitcast.141), calls=%async_computation.1 | async-start | bytes 8388608 | tf_op jit(solution)/shard_map/while
  125.2 1.8 copy-start.2
  128.4 1.5 copy-start.1
  129.9 2.7 copy-start
  136.3 7.0 %slice-start = ((s8[6291456]{0:T(1024)(128)(4,1)}), s8[2097152]{0:T(1024)(128)(4,1)S(1)}, s32[]{:S(2)}) async-start(s8[6291456]{0:T(1024)(128)(4,1)} %bitcast.141), calls=%async_computation | async-start | bytes 4194304 | tf_op jit(solution)/shard_map/while
  137.7 5.5 %slice-start.1 = ((s8[6291456]{0:T(1024)(128)(4,1)}), s8[4194304]{0:T(1024)(128)(4,1)S(1)}, s32[]{:S(2)}) async-start(s8[6291456]{0:T(1024)(128)(4,1)} %bitcast.141), calls=%async_computation.1 | async-start | bytes 8388608 | tf_op jit(solution)/shard_map/while
  146.6 1.8 copy-start.2
  149.7 1.5 copy-start.1
  151.2 2.7 copy-start
  157.6 6.9 %slice-start = ((s8[6291456]{0:T(1024)(128)(4,1)}), s8[2097152]{0:T(1024)(128)(4,1)S(1)}, s32[]{:S(2)}) async-start(s8[6291456]{0:T(1024)(128)(4,1)} %bitcast.141), calls=%async_computation | async-start | bytes 4194304 | tf_op jit(solution)/shard_map/while
  159.1 5.5 %slice-start.1 = ((s8[6291456]{0:T(1024)(128)(4,1)}), s8[4194304]{0:T(1024)(128)(4,1)S(1)}, s32[]{:S(2)}) async-start(s8[6291456]{0:T(1024)(128)(4,1)} %bitcast.141), calls=%async_computation.1 | async-start | bytes 8388608 | tf_op jit(solution)/shard_map/while
  168.0 1.8 copy-start.2
  172.6 2.7 copy-start
  179.0 7.0 %slice-start = ((s8[6291456]{0:T(1024)(128)(4,1)}), s8[2097152]{0:T(1024)(128)(4,1)S(1)}, s32[]{:S(2)}) async-start(s8[6291456]{0:T(1024)(128)(4,1)} %bitcast.141), calls=%async_computation | async-start | bytes 4194304 | tf_op jit(solution)/shard_map/while
  180.4 5.5 %slice-start.1 = ((s8[6291456]{0:T(1024)(128)(4,1)}), s8[4194304]{0:T(1024)(128)(4,1)S(1)}, s32[]{:S(2)}) async-start(s8[6291456]{0:T(1024)(128)(4,1)} %bitcast.141), calls=%async_computation.1 | async-start | bytes 8388608 | tf_op jit(solution)/shard_map/while
  189.4 1.8 copy-start.2
  194.0 2.7 copy-start
  200.4 6.9 %slice-start = ((s8[6291456]{0:T(1024)(128)(4,1)}), s8[2097152]{0:T(1024)(128)(4,1)S(1)}, s32[]{:S(2)}) async-start(s8[6291456]{0:T(1024)(128)(4,1)} %bitcast.141), calls=%async_computation | async-start | bytes 4194304 | tf_op jit(solution)/shard_map/while
  201.8 5.5 %slice-start.1 = ((s8[6291456]{0:T(1024)(128)(4,1)}), s8[4194304]{0:T(1024)(128)(4,1)S(1)}, s32[]{:S(2)}) async-start(s8[6291456]{0:T(1024)(128)(4,1)} %bitcast.141), calls=%async_computation.1 | async-start | bytes 8388608 | tf_op jit(solution)/shard_map/while
  210.7 1.8 copy-start.2
  213.9 5.1 %copy-start.3 = (f32[8,768,64]{1,2,0:T(8,128)S(1)}, f32[8,768,64]{1,2,0:T(8,128)}, u32[]{:S(2)}) copy-start(f32[8,768,64]{1,2,0:T(8,128)} %get-tuple-element.73) | copy-start | bytes 4718596
  215.5 8.2 %copy-start.4 = (bf16[8,8,256,64]{2,3,1,0:T(8,128)(2,1)S(1)}, bf16[8,8,256,64]{2,3,1,0:T(8,128)(2,1)}, u32[]{:S(2)}) copy-start(bf16[8,8,256,64]{2,3,1,0:T(8,128)(2,1)} %get-tuple-element.71) | copy-start | bytes 6291460
  216.4 105.5 %collective-permute-start.6 = (bf16[256,512]{0,1:T(8,128)(2,1)}, bf16[256,512]{0,1:T(8,128)(2,1)S(1)}, u32[]{:S(2)}, u32[]{:S(2)}) collective-permute-start(bf16[256,512]{0,1:T(8,128)(2,1)} %bitcast.26), channel_id=1, source_target_pairs={{1,0},{2,1},{3,2},{4,3},{5,4},{6,5},{7,6},{8,7},{9,8},{10,9},{11,1... | collective-permute-start | bytes 786440 | tf_op jit(solution)/shard_map/ppermute | solution.py:18
  217.7 104.2 %collective-permute-start.7 = (bf16[256,512]{0,1:T(8,128)(2,1)}, bf16[256,512]{0,1:T(8,128)(2,1)}, u32[]{:S(2)}, u32[]{:S(2)}) collective-permute-start(bf16[256,512]{0,1:T(8,128)(2,1)} %bitcast.27), channel_id=1, source_target_pairs={{2,0},{3,1},{4,2},{5,3},{6,4},{7,5},{8,6},{9,7},{10,8},{11,9},{12,... | collective-permute-start | bytes 786440 | tf_op jit(solution)/shard_map/ppermute | solution.py:18
  219.9 103.9 %collective-permute-start.4 = (bf16[256,512]{0,1:T(8,128)(2,1)}, bf16[256,512]{0,1:T(8,128)(2,1)}, u32[]{:S(2)}, u32[]{:S(2)}) collective-permute-start(bf16[256,512]{0,1:T(8,128)(2,1)} %bitcast.21), channel_id=1, source_target_pairs={{1,0},{2,1},{3,2},{4,3},{5,4},{6,5},{7,6},{8,7},{9,8},{10,9},{11,1... | collective-permute-start | bytes 786440 | tf_op jit(solution)/shard_map/ppermute | solution.py:18
  221.2 102.6 %collective-permute-start.5 = (bf16[256,512]{0,1:T(8,128)(2,1)}, bf16[256,512]{0,1:T(8,128)(2,1)}, u32[]{:S(2)}, u32[]{:S(2)}) collective-permute-start(bf16[256,512]{0,1:T(8,128)(2,1)} %bitcast.22), channel_id=1, source_target_pairs={{2,0},{3,1},{4,2},{5,3},{6,4},{7,5},{8,6},{9,7},{10,8},{11,9},{12,... | collective-permute-start | bytes 786440 | tf_op jit(solution)/shard_map/ppermute | solution.py:18
  (4 other events, 6.0 us)
where the time goes:
time: 327 us; the launch traced here: 326 us
  matrix products  136 us (42%)
  blocking collectives  91.2 us (28%)
  local copies, waits for them, and re-layouts  33.3 us (10%)
  other arithmetic  33.1 us (10%)
  starting transfers between devices  22.3 us (7%)
  waiting for transfers between devices  8.56 us (3%)
    psum x1, blocking collectives, on_device(): sink_total = lax.psum(sink_grad, ('dp', 'ctx'))  91.2 us
    dot_general x8, matrix products, head_block(): jnp.einsum('gtl,gtd->ld', weights, g_head, preferred_element_type=jnp.flo...  44 us
    dot_general x8, matrix products, head_block(): jnp.einsum('gtl,ld->gtd', weights, v_head, preferred_element_type=jnp.flo...  29.8 us
    dot_general x8, matrix products, head_block(): jnp.einsum('gtd,ld->gtl', g_head, v_head, preferred_element_type=jnp.floa...  27.2 us
    ppermute x8, starting transfers between devices, passed_along(): return lax.ppermute(block, axis, route)  22.3 us
    unnamed x16, local copies, waits for them, and re-layouts  18.2 us
    dot_general x8, matrix products, head_block(): jnp.einsum('gtl,ld->gtd', score_grads, k_head, preferred_element_type=jnp...  14.3 us
    reduce_sum x8, other arithmetic, head_block(): denom = jnp.sum(expo, axis=-1) + sink_part  12.5 us
  transfers between devices with their start and end apart: 8, of which 1 were waited for; matrix products, arithmetic and copies ran while one was open for 7% of the time, Pallas kernels for 0%

commit v1 on v0

v1 whole, which is shorter than its diff:
```python
import functools

import jax
import jax.numpy as jnp
from jax import lax
from jax.experimental import pallas as pl
from jax.experimental.pallas import tpu as pltpu
from jax.sharding import PartitionSpec as P

H = 64
KV = 8
HD = 64
SPAN = 2
ROWS = 256
TILE = 128
WIN = SPAN * ROWS + TILE
CHUNKS = 2
PAIRS = KV // 2
FAR = 16384.0

score_scale = 0.125


def passed_along(block, axis, distance):
    devices = range(lax.axis_size(axis))
    route = [(i - distance, i) for i in devices if i - distance in devices]
    return lax.ppermute(block, axis, route)


def dot(a, b, dim_a, dim_b):
    return lax.dot_general(
        a, b, (((dim_a,), (dim_b,)), ((), ())), preferred_element_type=jnp.float32
    )


def side_by_side(x):
    return jnp.concatenate([x[:HD], x[HD:]], axis=1)


def stacked(x):
    return jnp.concatenate([x[:, :TILE], x[:, TILE:]], axis=0)


def kernel(first, *refs):
    if not first:
        refs = refs[:8] + refs[10:]
    (q_ref, g_ref, kv2_ref, kv1_ref, kv0_ref, f_ref, t_ref, s_ref) = refs[:8]
    (o_ref, dq_ref, d2_ref, d1_ref, d0_ref, sg_ref) = refs[8:14]
    (kk, vv, kt, vt, pt, dst, qm, gm, acck, accv) = refs[14:]
    lane = lax.broadcasted_iota(jnp.int32, (TILE, 2 * HD), 1)
    even = lane < HD
    key_at = lax.broadcasted_iota(jnp.int32, (TILE, 2 * TILE), 0)
    query_at = lax.broadcasted_iota(jnp.int32, (TILE, 2 * TILE), 1) % TILE
    causal = key_at <= query_at
    for n, ref in enumerate((kv2_ref, kv1_ref, kv0_ref)):
        kt[:, n * ROWS : (n + 1) * ROWS] = ref[:, : 2 * HD].T
        vt[:, n * ROWS : (n + 1) * ROWS] = ref[:, 2 * HD :].T
    kk[:, 2 * HD :] = t_ref[...]
    for h in range(2):
        for n, ref in enumerate((kv2_ref, kv1_ref, kv0_ref)):
            k_head = ref[:, h * HD : (h + 1) * HD]
            v_head = ref[:, (2 + h) * HD : (3 + h) * HD]
            rows = slice(n * ROWS, (n + 1) * ROWS)
            kk[rows, :HD] = k_head
            kk[rows, HD : 2 * HD] = k_head
            vv[rows, :HD] = v_head
            vv[rows, HD:] = v_head
        own = slice(h * HD, (h + 1) * HD)
        for r in range(ROWS // TILE):
            rows = slice(r * TILE, (r + 1) * TILE)
            win = slice(r * TILE, r * TILE + WIN)
            f = f_ref[rows, :]
            for p in range(4):
                lanes = slice(h * 512 + p * 128, h * 512 + (p + 1) * 128)
                cols = slice(p * 2 * TILE, (p + 1) * 2 * TILE)
                line = slice(h * 4 + p, h * 4 + p + 1)
                qp = q_ref[rows, lanes] * jnp.bfloat16(score_scale)
                gp = g_ref[rows, lanes]
                zero = jnp.zeros_like(qp)
                rq = jnp.concatenate([jnp.where(even, qp, zero), jnp.where(even, zero, qp)], 0)
                rg = jnp.concatenate([jnp.where(even, gp, zero), jnp.where(even, zero, gp)], 0)
                rqf = jnp.concatenate([rq, jnp.concatenate([f, f], 0)], 1)
                s = dot(kk[win, :], rqf, 1, 1)
                s = jnp.concatenate(
                    [s[: WIN - TILE], jnp.where(causal, s[WIN - TILE :], -FAR)], 0
                )
                sink = s_ref[line, :]
                top = jnp.maximum(jnp.max(s, axis=0, keepdims=True), sink)
                expo = jnp.exp(s - top)
                sink_part = jnp.exp(sink - top)
                share = 1.0 / (jnp.sum(expo, axis=0, keepdims=True) + sink_part)
                probs = expo * share
                weights = probs.astype(jnp.bfloat16)
                pt[:, cols] = weights
                out = dot(vt[own, win], weights, 1, 0).astype(jnp.bfloat16)
                out = out.astype(jnp.float32)
                g_t = side_by_side(gp.astype(jnp.float32).T)
                rowdot = jnp.sum(g_t * out, axis=0, keepdims=True)
                o_ref[rows, lanes] = stacked(out).T.astype(jnp.bfloat16)
                dp = dot(vv[win, :], rg, 1, 1)
                ds = (probs * (dp - rowdot)).astype(jnp.bfloat16)
                dst[:, cols] = ds
                dq = dot(kt[own, win], ds, 1, 0) * score_scale
                dq_ref[rows, lanes] = stacked(dq).T.astype(jnp.bfloat16)
                sink_grad = -(sink_part * share * rowdot)
                if r == 0:
                    sg_ref[line, :] = sink_grad
                else:
                    sg_ref[line, :] += sink_grad
                qm[cols, :] = rq
                gm[cols, :] = rg
            for acc, big, small in ((acck, dst, qm), (accv, pt, gm)):
                part = dot(big[...], small[...], 1, 0)
                if r == 0:
                    acc[h, :WIN, :] = part
                else:
                    acc[h, TILE:WIN, :] += part[: WIN - TILE]
                    acc[h, WIN:, :] = part[WIN - TILE :]
    lane = lax.broadcasted_iota(jnp.int32, (ROWS, 2 * HD), 1)
    for side, acc in ((0, acck), (1, accv)):
        cols = slice(side * 2 * HD, (side + 1) * 2 * HD)
        for n, ref in enumerate((d2_ref, d1_ref, d0_ref)):
            a = acc[0, n * ROWS : (n + 1) * ROWS, :]
            b = acc[1, n * ROWS : (n + 1) * ROWS, :]
            a = a + pltpu.roll(a, HD, 1)
            b = b + pltpu.roll(b, HD, 1)
            ref[:, cols] = jnp.where(lane < HD, a, b).astype(ref.dtype)


def attend(chunk, queries, grads, kv, f, t, sink_rows, so_far):
    bf, f32 = jnp.bfloat16, jnp.float32
    steps = PAIRS // CHUNKS
    base = chunk * steps
    wide = pl.BlockSpec((ROWS, 1024), lambda i: (0, base + i))
    pair = pl.BlockSpec((ROWS, 256), lambda i: (0, i))
    small = pl.BlockSpec((8, 256), lambda i: (base + i, 0))
    whole = pl.BlockSpec(memory_space=pl.ANY)
    in_specs = [wide, wide, pair, pair, pair]
    in_specs += [pl.BlockSpec((ROWS, 128), lambda i: (0, 0))]
    in_specs += [pl.BlockSpec((3 * ROWS, 128), lambda i: (0, 0)), small]
    args = (queries, grads, *kv, f, t, sink_rows)
    aliases = {}
    if so_far is not None:
        in_specs += [whole, whole]
        args += so_far
        aliases = {8: 0, 9: 1}
    return pl.pallas_call(
        functools.partial(kernel, so_far is None),
        grid=(steps,),
        in_specs=in_specs,
        out_specs=[wide, wide, pair, pair, pair, pl.BlockSpec((8, 256), lambda i: (i, 0))],
        out_shape=[
            jax.ShapeDtypeStruct((ROWS, H * HD), bf),
            jax.ShapeDtypeStruct((ROWS, H * HD), bf),
            jax.ShapeDtypeStruct((ROWS, 256 * steps), bf),
            jax.ShapeDtypeStruct((ROWS, 256 * steps), f32),
            jax.ShapeDtypeStruct((ROWS, 256 * steps), f32),
            jax.ShapeDtypeStruct((8 * steps, 256), f32),
        ],
        scratch_shapes=[
            pltpu.VMEM((3 * ROWS, 256), bf),
            pltpu.VMEM((3 * ROWS, 128), bf),
            pltpu.VMEM((128, 3 * ROWS), bf),
            pltpu.VMEM((128, 3 * ROWS), bf),
            pltpu.VMEM((WIN, 1024), bf),
            pltpu.VMEM((WIN, 1024), bf),
            pltpu.VMEM((1024, 128), bf),
            pltpu.VMEM((1024, 128), bf),
            pltpu.VMEM((2, 3 * ROWS, 128), f32),
            pltpu.VMEM((2, 3 * ROWS, 128), f32),
        ],
        input_output_aliases=aliases,
        compiler_params=pltpu.CompilerParams(vmem_limit_bytes=48 * 1024 * 1024),
    )(*args)


def on_device(query, key_proj, value, sinks, doc_ids, grad_out):
    queries, keys, values, grads = query[0], key_proj[0], value[0], grad_out[0]
    steps = PAIRS // CHUNKS
    own = []
    for c in range(CHUNKS):
        parts = []
        for i in range(c * steps, (c + 1) * steps):
            parts += [keys[:, i * 128 : (i + 1) * 128], values[:, i * 128 : (i + 1) * 128]]
        own.append(jnp.concatenate(parts, axis=1))
    near = [passed_along(x, "ctx", 1) for x in own]
    far = [passed_along(x, "ctx", 1) for x in near]

    start = lax.axis_index("ctx") * ROWS
    front = SPAN * ROWS
    seg_pad = jnp.concatenate([jnp.full((front,), -1, jnp.int32), doc_ids[0]], axis=0)
    k_seg = lax.dynamic_slice_in_dim(seg_pad, start, front + ROWS)
    q_seg = k_seg[front:]
    feature = jnp.arange(128, dtype=jnp.int32)[None, :]
    f = ((feature <= q_seg[:, None]) & (feature < 64)).astype(jnp.bfloat16)
    t = jnp.where((feature > k_seg[:, None]) & (feature < 64), -FAR, 0.0).astype(jnp.bfloat16)
    sink_rows = jnp.repeat(sinks, TILE).reshape(H // 2, 2 * TILE)

    so_far, nearest, sums, sink_sums = None, [], [], []
    for c in range(CHUNKS):
        attended, grad_q, d2, d1, d0, sg = attend(
            c, queries, grads, (far[c], near[c], own[c]), f, t, sink_rows, so_far
        )
        so_far = (attended, grad_q)
        got = passed_along(d2, "ctx", -1).astype(jnp.float32)
        nearest.append((d1 + got).astype(jnp.bfloat16))
        sums.append(d0)
        sink_sums.append(jnp.sum(sg.reshape(-1, TILE), axis=1))
    grad_k, grad_v = [], []
    for c in range(CHUNKS):
        total = sums[c] + passed_along(nearest[c], "ctx", -1).astype(jnp.float32)
        total = total.astype(jnp.bfloat16)
        for i in range(steps):
            grad_k.append(total[:, i * 256 : i * 256 + 128])
            grad_v.append(total[:, i * 256 + 128 : (i + 1) * 256])
    sink_grad = jnp.concatenate(sink_sums)
    devices = lax.axis_size("dp") * lax.axis_size("ctx")
    spread = jnp.broadcast_to(sink_grad[None], (devices, H))
    sink_total = jnp.sum(lax.all_to_all(spread, ("dp", "ctx"), 0, 0, tiled=True), axis=0)
    return (
        attended[None],
        grad_q[None],
        jnp.concatenate(grad_k, axis=1)[None],
        jnp.concatenate(grad_v, axis=1)[None],
        sink_total,
    )


def solution(mesh):
    in_specs = (
        P("dp", "ctx", None),
        P("dp", "ctx", None),
        P("dp", "ctx", None),
        P(),
        P("dp", None),
        P("dp", "ctx", None),
    )
    out_specs = (
        P("dp", "ctx", None),
        P("dp", "ctx", None),
        P("dp", "ctx", None),
        P("dp", "ctx", None),
        P(),
    )
    return jax.shard_map(
        on_device, mesh=mesh, in_specs=in_specs, out_specs=out_specs, check_vma=False
    )
```

time: 327 us -> 154 us (0.47)
  the two profiles are of different devices: /device:TPU:1 before, /device:TPU:24 now
where the time goes in v1:
time: 154 us; the launch traced here: 153 us
  Pallas kernels  65.6 us (43%)
  starting transfers between devices  42.6 us (28%)
  waiting for transfers between devices  31.5 us (20%)
  local copies, waits for them, and re-layouts  7.43 us (5%)
  other arithmetic  5.27 us (3%)
    pallas_call x2, Pallas kernels, attend(): pl.pallas_call(functools.partial(kernel, so_far is None), grid=(steps,),...  65.6 us
    ppermute x8, starting transfers between devices, passed_along(): return lax.ppermute(block, axis, route)  36 us
    ppermute x8, waiting for transfers between devices, passed_along(): return lax.ppermute(block, axis, route)  31.5 us
    all_to_all x1, starting transfers between devices, on_device(): lax.all_to_all(spread, ('dp', 'ctx'), 0, 0, tiled=True)  6.62 us
    unnamed x25, local copies, waits for them, and re-layouts  5.05 us
  transfers between devices with their start and end apart: 9, of which 5 were waited for; matrix products, arithmetic and copies ran while one was open for 3% of the time, Pallas kernels for 21%

profile of v1, /device:TPU:24, one launch (start us, length us, event | category | flops | bytes accessed | tf_op | source)
XLA Modules:
  0.0 153.3 jit_solution(6764070778530101173)
XLA Ops:
  0.6 0.0 copy-start.10
  0.6 0.0 copy-start.11
  0.7 0.0 copy-start
  0.7 1.3 fusion.5
  2.0 3.8 %collective-permute-start = (bf16[256,512]{1,0:T(8,128)(2,1)S(1)}, bf16[256,512]{1,0:T(8,128)(2,1)S(1)}, u32[]{:S(2)}, u32[]{:S(2)}) collective-permute-start(bf16[256,512]{1,0:T(8,128)(2,1)S(1)} %pad_maximum_fusion.refs_4_), channel_id=1, source_target_pairs={{0,1},{1,2},{2,3},{3,4},{4,5},{5,6},{6,7},{7,8},{8,9},{9,10},{10,1... | collective-permute-start | bytes 786440 | tf_op jit(solution)/shard_map/ppermute | solution.py:27
  5.8 3.8 %collective-permute-start.2 = (bf16[256,512]{1,0:T(8,128)(2,1)S(1)}, bf16[256,512]{1,0:T(8,128)(2,1)S(1)}, u32[]{:S(2)}, u32[]{:S(2)}) collective-permute-start(bf16[256,512]{1,0:T(8,128)(2,1)S(1)} %pad_maximum_fusion.1.refs_4_), channel_id=1, source_target_pairs={{0,1},{1,2},{2,3},{3,4},{4,5},{5,6},{6,7},{7,8},{8,9},{9,10},{10,1... | collective-permute-start | bytes 786440 | tf_op jit(solution)/shard_map/ppermute | solution.py:27
  9.7 0.1 pad_dynamic-slice_fusion
  9.8 9.9 %collective-permute-done.refs_3_ = bf16[256,512]{1,0:T(8,128)(2,1)S(1)} collective-permute-done((bf16[256,512]{1,0:T(8,128)(2,1)S(1)}, bf16[256,512]{1,0:T(8,128)(2,1)S(1)}, u32[]{:S(2)}, u32[]{:S(2)}) %collective-permute-start) | collective-permute-done | bytes 262176 | tf_op jit(solution)/shard_map/ppermute | solution.py:27
  19.7 1.9 %collective-permute-start.1 = (bf16[256,512]{1,0:T(8,128)(2,1)S(1)}, bf16[256,512]{1,0:T(8,128)(2,1)}, u32[]{:S(2)}, u32[]{:S(2)}) collective-permute-start(bf16[256,512]{1,0:T(8,128)(2,1)S(1)} %collective-permute-done.refs_3_), channel_id=1, source_target_pairs={{0,1},{1,2},{2,3},{3,4},{4,5},{5,6},{6,7},{7,8},{8,9},{9,10},{10,1... | collective-permute-start | bytes 786440 | tf_op jit(solution)/shard_map/ppermute | solution.py:27
  21.6 2.9 %collective-permute-done.2.refs_3_ = bf16[256,512]{1,0:T(8,128)(2,1)S(1)} collective-permute-done((bf16[256,512]{1,0:T(8,128)(2,1)S(1)}, bf16[256,512]{1,0:T(8,128)(2,1)S(1)}, u32[]{:S(2)}, u32[]{:S(2)}) %collective-permute-start.2) | collective-permute-done | bytes 262176 | tf_op jit(solution)/shard_map/ppermute | solution.py:27
  24.5 1.9 %collective-permute-start.3 = (bf16[256,512]{1,0:T(8,128)(2,1)S(1)}, bf16[256,512]{1,0:T(8,128)(2,1)S(1)}, u32[]{:S(2)}, u32[]{:S(2)}) collective-permute-start(bf16[256,512]{1,0:T(8,128)(2,1)S(1)} %collective-permute-done.2.refs_3_), channel_id=1, source_target_pairs={{0,1},{1,2},{2,3},{3,4},{4,5},{5,6},{6,7},{7,8},{8,9},{9,10},{10,1... | collective-permute-start | bytes 786440 | tf_op jit(solution)/shard_map/ppermute | solution.py:27
  26.4 0.1 fusion.2.refs_5_
  26.5 0.0 copy-done.11
  26.6 0.1 broadcast_in_dim.39
  26.7 0.1 broadcast_in_dim.40
  26.8 0.2 select_convert_fusion.refs_6_
  26.9 12.7 %collective-permute-done.3.refs_2_ = bf16[256,512]{1,0:T(8,128)(2,1)S(1)} collective-permute-done((bf16[256,512]{1,0:T(8,128)(2,1)S(1)}, bf16[256,512]{1,0:T(8,128)(2,1)S(1)}, u32[]{:S(2)}, u32[]{:S(2)}) %collective-permute-start.3) | collective-permute-done | bytes 262176 | tf_op jit(solution)/shard_map/ppermute | solution.py:27
  39.6 0.7 copy-done.7
  40.3 0.0 copy-done
  40.3 0.9 copy-done.6
  41.3 0.9 copy-done.8
  42.2 32.8 %shard_map.101 = (bf16[256,4096]{1,0:T(8,128)(2,1)}, bf16[256,4096]{1,0:T(8,128)(2,1)}, bf16[256,512]{1,0:T(8,128)(2,1)S(1)}, f32[256,512]{1,0:T(8,128)S(1)}, f3...) custom-call(bf16[256,4096]{1,0:T(8,128)(2,1)S(1)} %bitcast.15, bf16[256,4096]{1,0:T(8,128)(2,1)} %bitcast.19, ...), custom_call_target="tpu_custom_call" | custom-call | tf_op jit(solution)/shard_map/pallas_call | solution.py:147
  75.0 0.8 copy-done.1
  75.8 0.0 collective-permute-done.1.refs_2_
  75.8 32.8 %shard_map.102 = (bf16[256,4096]{1,0:T(8,128)(2,1)}, bf16[256,4096]{1,0:T(8,128)(2,1)}, bf16[256,512]{1,0:T(8,128)(2,1)}, f32[256,512]{1,0:T(8,128)S(1)}, f32[256,512]{1,0:T(8,128)S(1)}, /*index=5*/f32[16,256]{1,0:T(8,128)S(1)}) custom-call(bf16[256,4096]{1,0:T(8,128)(2,1)S(1)} %bitcast.16, ...), custom_call_target="tpu_custom_call", output_to_operand_aliasing={{0}: (8, {}), {1}: (9, {})} | custom-call | tf_op jit(solution)/shard_map/pallas_call | solution.py:147
  108.7 0.8 copy-done.2
  109.5 0.8 copy-done.4
  110.3 2.0 %collective-permute-start.6 = (bf16[256,512]{1,0:T(8,128)(2,1)}, bf16[256,512]{1,0:T(8,128)(2,1)S(1)}, u32[]{:S(2)}, u32[]{:S(2)}) collective-permute-start(bf16[256,512]{1,0:T(8,128)(2,1)} %get-tuple-element.26), channel_id=1, source_target_pairs={{1,0},{2,1},{3,2},{4,3},{5,4},{6,5},{7,6},{8,7},{9,8},{10,9},{11,1... | collective-permute-start | bytes 786440 | tf_op jit(solution)/shard_map/ppermute | solution.py:27
  112.3 0.1 reduce_sum.27
  112.5 0.1 reduce_sum.28
  112.6 0.1 pad_maximum_fusion.2
  112.6 0.7 broadcast_in_dim.46
  113.4 6.6 %all-to-all-start = ((f32[256,1,64]{2,1,0:T(1,128)}), f32[256,1,64]{2,1,0:T(1,128)S(1)}, u32[]{:S(2)}, u32[]{:S(2)}) async-start(f32[256,1,64]{2,1,0:T(1,128)} %broadcast_in_dim.46), calls=%async_computation | async-start | bytes 262144 | tf_op jit(solution)/shard_map/all_to_all | solution.py:219
  120.0 9.4 %collective-permute-start.4 = (bf16[256,512]{1,0:T(8,128)(2,1)}, bf16[256,512]{1,0:T(8,128)(2,1)S(1)}, u32[]{:S(2)}, u32[]{:S(2)}) collective-permute-start(bf16[256,512]{1,0:T(8,128)(2,1)} %copy-done.9), channel_id=1, source_target_pairs={{1,0},{2,1},{3,2},{4,3},{5,4},{6,5},{7,6},{8,7},{9,8},{10,9},{11,1... | collective-permute-start | bytes 786440 | tf_op jit(solution)/shard_map/ppermute | solution.py:27
  129.4 0.0 collective-permute-done.6
  129.4 1.1 add_convert_fusion.1
  130.5 3.1 %collective-permute-start.7 = (bf16[256,512]{1,0:T(8,128)(2,1)S(1)}, bf16[256,512]{1,0:T(8,128)(2,1)S(1)}, u32[]{:S(2)}, u32[]{:S(2)}) collective-permute-start(bf16[256,512]{1,0:T(8,128)(2,1)S(1)} %add_convert_fusion.1), channel_id=1, source_target_pairs={{1,0},{2,1},{3,2},{4,3},{5,4},{6,5},{7,6},{8,7},{9,8},{10,9},{11,1... | collective-permute-start | bytes 786440 | tf_op jit(solution)/shard_map/ppermute | solution.py:27
  133.6 0.0 all-to-all-done
  133.6 0.8 reduce_sum.29
  134.4 1.9 %collective-permute-done.4 = bf16[256,512]{1,0:T(8,128)(2,1)S(1)} collective-permute-done((bf16[256,512]{1,0:T(8,128)(2,1)}, bf16[256,512]{1,0:T(8,128)(2,1)S(1)}, u32[]{:S(2)}, u32[]{:S(2)}) %collective-permute-start.4) | collective-permute-done | bytes 262176 | tf_op jit(solution)/shard_map/ppermute | solution.py:27
  136.4 1.1 add_convert_fusion.3
  137.5 10.0 %collective-permute-start.5 = (bf16[256,512]{1,0:T(8,128)(2,1)S(1)}, bf16[256,512]{1,0:T(8,128)(2,1)S(1)}, u32[]{:S(2)}, u32[]{:S(2)}) collective-permute-start(bf16[256,512]{1,0:T(8,128)(2,1)S(1)} %add_convert_fusion.3), channel_id=1, source_target_pairs={{1,0},{2,1},{3,2},{4,3},{5,4},{6,5},{7,6},{8,7},{9,8},{10,9},{11,1... | collective-permute-start | bytes 786440 | tf_op jit(solution)/shard_map/ppermute | solution.py:27
  147.5 0.0 collective-permute-done.7
  147.5 0.1 add_convert_fusion
  147.6 4.1 %collective-permute-done.5 = bf16[256,512]{1,0:T(8,128)(2,1)S(1)} collective-permute-done((bf16[256,512]{1,0:T(8,128)(2,1)S(1)}, bf16[256,512]{1,0:T(8,128)(2,1)S(1)}, u32[]{:S(2)}, u32[]{:S(2)}) %collective-permute-start.5) | collective-permute-done | bytes 262176 | tf_op jit(solution)/shard_map/ppermute | solution.py:27
  151.7 0.1 add_convert_fusion.2
  151.9 0.7 maximum_bitcast_fusion.1
  152.6 0.7 maximum_bitcast_fusion
  (22 shorter events, 0.2 us)
Async XLA Ops:
  0.6 9.1 %copy-start.10 = (s32[1,16384]{1,0:T(1,128)S(1)}, s32[1,16384]{1,0:T(1,128)}, u32[]{:S(2)}) copy-start(s32[1,16384]{1,0:T(1,128)} %param.10) | copy-start | bytes 196612
  0.6 25.9 %copy-start.11 = (f32[64]{0:T(128)S(1)}, f32[64]{0:T(128)}, u32[]{:S(2)}) copy-start(f32[64]{0:T(128)} %param.9) | copy-start | bytes 772
  0.7 39.7 %copy-start = (bf16[1,256,4096]{2,1,0:T(8,128)(2,1)S(1)}, bf16[1,256,4096]{2,1,0:T(8,128)(2,1)}, u32[]{:S(2)}) copy-start(bf16[1,256,4096]{2,1,0:T(8,128)(2,1)} %param.6) | copy-start | bytes 6291460
  2.0 17.8 %collective-permute-start = (bf16[256,512]{1,0:T(8,128)(2,1)S(1)}, bf16[256,512]{1,0:T(8,128)(2,1)S(1)}, u32[]{:S(2)}, u32[]{:S(2)}) collective-permute-start(bf16[256,512]{1,0:T(8,128)(2,1)S(1)} %pad_maximum_fusion.refs_4_), channel_id=1, source_target_pairs={{0,1},{1,2},{2,3},{3,4},{4,5},{5,6},{6,7},{7,8},{8,9},{9,10},{10,1... | collective-permute-start | bytes 786440 | tf_op jit(solution)/shard_map/ppermute | solution.py:27
  5.8 18.7 %collective-permute-start.2 = (bf16[256,512]{1,0:T(8,128)(2,1)S(1)}, bf16[256,512]{1,0:T(8,128)(2,1)S(1)}, u32[]{:S(2)}, u32[]{:S(2)}) collective-permute-start(bf16[256,512]{1,0:T(8,128)(2,1)S(1)} %pad_maximum_fusion.1.refs_4_), channel_id=1, source_target_pairs={{0,1},{1,2},{2,3},{3,4},{4,5},{5,6},{6,7},{7,8},{8,9},{9,10},{10,1... | collective-permute-start | bytes 786440 | tf_op jit(solution)/shard_map/ppermute | solution.py:27
  19.7 56.1 %collective-permute-start.1 = (bf16[256,512]{1,0:T(8,128)(2,1)S(1)}, bf16[256,512]{1,0:T(8,128)(2,1)}, u32[]{:S(2)}, u32[]{:S(2)}) collective-permute-start(bf16[256,512]{1,0:T(8,128)(2,1)S(1)} %collective-permute-done.refs_3_), channel_id=1, source_target_pairs={{0,1},{1,2},{2,3},{3,4},{4,5},{5,6},{6,7},{7,8},{8,9},{9,10},{10,1... | collective-permute-start | bytes 786440 | tf_op jit(solution)/shard_map/ppermute | solution.py:27
  24.5 15.8 %copy-start.5 = (bf16[256,512]{1,0:T(8,128)(2,1)}, bf16[256,512]{1,0:T(8,128)(2,1)S(1)}, u32[]{:S(2)}) copy-start(bf16[256,512]{1,0:T(8,128)(2,1)S(1)} %collective-permute-done.2.refs_3_) | copy-start | bytes 786436
  24.5 15.1 %collective-permute-start.3 = (bf16[256,512]{1,0:T(8,128)(2,1)S(1)}, bf16[256,512]{1,0:T(8,128)(2,1)S(1)}, u32[]{:S(2)}, u32[]{:S(2)}) collective-permute-start(bf16[256,512]{1,0:T(8,128)(2,1)S(1)} %collective-permute-done.2.refs_3_), channel_id=1, source_target_pairs={{0,1},{1,2},{2,3},{3,4},{4,5},{5,6},{6,7},{7,8},{8,9},{9,10},{10,1... | collective-permute-start | bytes 786440 | tf_op jit(solution)/shard_map/ppermute | solution.py:27
  39.6 0.7 copy-start.7
  40.3 1.0 copy-start.6
  41.3 0.9 copy-start.8
  75.0 0.8 copy-start.1
  75.8 32.9 %copy-start.9 = (bf16[256,512]{1,0:T(8,128)(2,1)}, bf16[256,512]{1,0:T(8,128)(2,1)S(1)}, u32[]{:S(2)}) copy-start(bf16[256,512]{1,0:T(8,128)(2,1)S(1)} %get-tuple-element.23) | copy-start | bytes 786436
  108.6 0.8 copy-start.2
  109.4 0.8 copy-start.4
  110.3 37.2 %copy-start.3 = (f32[256,512]{1,0:T(8,128)S(1)}, f32[256,512]{1,0:T(8,128)}, u32[]{:S(2)}) copy-start(f32[256,512]{1,0:T(8,128)} %copy-done.2) | copy-start | bytes 1572868
  110.3 19.1 %collective-permute-start.6 = (bf16[256,512]{1,0:T(8,128)(2,1)}, bf16[256,512]{1,0:T(8,128)(2,1)S(1)}, u32[]{:S(2)}, u32[]{:S(2)}) collective-permute-start(bf16[256,512]{1,0:T(8,128)(2,1)} %get-tuple-element.26), channel_id=1, source_target_pairs={{1,0},{2,1},{3,2},{4,3},{5,4},{6,5},{7,6},{8,7},{9,8},{10,9},{11,1... | collective-permute-start | bytes 786440 | tf_op jit(solution)/shard_map/ppermute | solution.py:27
  113.4 20.3 %all-to-all-start = ((f32[256,1,64]{2,1,0:T(1,128)}), f32[256,1,64]{2,1,0:T(1,128)S(1)}, u32[]{:S(2)}, u32[]{:S(2)}) async-start(f32[256,1,64]{2,1,0:T(1,128)} %broadcast_in_dim.46), calls=%async_computation | async-start | bytes 262144 | tf_op jit(solution)/shard_map/all_to_all | solution.py:219
  120.0 16.4 %collective-permute-start.4 = (bf16[256,512]{1,0:T(8,128)(2,1)}, bf16[256,512]{1,0:T(8,128)(2,1)S(1)}, u32[]{:S(2)}, u32[]{:S(2)}) collective-permute-start(bf16[256,512]{1,0:T(8,128)(2,1)} %copy-done.9), channel_id=1, source_target_pairs={{1,0},{2,1},{3,2},{4,3},{5,4},{6,5},{7,6},{8,7},{9,8},{10,9},{11,1... | collective-permute-start | bytes 786440 | tf_op jit(solution)/shard_map/ppermute | solution.py:27
  130.5 17.0 %collective-permute-start.7 = (bf16[256,512]{1,0:T(8,128)(2,1)S(1)}, bf16[256,512]{1,0:T(8,128)(2,1)S(1)}, u32[]{:S(2)}, u32[]{:S(2)}) collective-permute-start(bf16[256,512]{1,0:T(8,128)(2,1)S(1)} %add_convert_fusion.1), channel_id=1, source_target_pairs={{1,0},{2,1},{3,2},{4,3},{5,4},{6,5},{7,6},{8,7},{9,8},{10,9},{11,1... | collective-permute-start | bytes 786440 | tf_op jit(solution)/shard_map/ppermute | solution.py:27
  137.5 14.3 %collective-permute-start.5 = (bf16[256,512]{1,0:T(8,128)(2,1)S(1)}, bf16[256,512]{1,0:T(8,128)(2,1)S(1)}, u32[]{:S(2)}, u32[]{:S(2)}) collective-permute-start(bf16[256,512]{1,0:T(8,128)(2,1)S(1)} %add_convert_fusion.3), channel_id=1, source_target_pairs={{1,0},{2,1},{3,2},{4,3},{5,4},{6,5},{7,6},{8,7},{9,8},{10,9},{11,1... | collective-permute-start | bytes 786440 | tf_op jit(solution)/shard_map/ppermute | solution.py:27
